TPU v7x, 32 devices: a whole 2x2x4 slice. The times are simulated.
32 devices in a mesh: dp: 8 (over z, core), tensor: 2 (over y), mp: 2 (over x).
Axes of the slice: x: 2, y: 2, z: 4, core: 2. Of those that a mesh axis runs over, the one named last changes fastest.
Arguments:
- step_embeds: bfloat16 [2, 256, 32, 8192], P('mp', 'dp', None, 'tensor'), may hold values from -6 to 6
- step_len: int32 [256], replicated, may hold values from 8 to 32, as said below
- leaf_of_step: int32 [256], replicated, may hold values from 0 to 31, as said below
- cache_len: int32 [32], P('dp'), may hold values from 96 to 768, as said below
- caches: bfloat16 [2, 32, 768, 2048], P('mp', 'dp', None, 'tensor'), may hold values from -500 to 500
- norm_gain: float32 [2, 8192], P('mp'), may hold values from 0.1 to 1.9
- qkv_weight: bfloat16 [2, 8192, 6144], P('mp', 'dp', 'tensor'), may hold values from -0.1875 to 0.1875
- score_weight: float32 [2, 4096], P('mp', 'tensor'), may hold values from -0.09375 to 0.09375
Outputs:
- contexts: bfloat16 [2, 32, 8, 32, 4096], P('mp', 'dp', None, None, 'tensor')
- step_value: float32 [32, 8], P('dp')
Inputs may be any that keep to these rules, and one draw needn't show every extreme that they name: `leaf_of_step`: every leaf is named by exactly 8 steps, and each aligned block of 32 steps names the leaves of every aligned block of 4 leaves equally often. `step_len`: some step has all 32 tokens. `cache_len`: some leaf fills all 768 cache positions.
All inputs are finite; a program needn't handle non-finite values.
Results may differ from a plain program's by a relative error of at most 0.0049.
The roundings to bfloat16 on the way count: a program that leaves them out, or rounds other values in their place, can miss the bound.
Values may be sent and summed in bfloat16 or wider, within the bound.
A program may use at most 192 MiB of HBM per device.

v0:
```python
import jax
import jax.numpy as jnp
from jax import lax
from jax.sharding import PartitionSpec as P

KVH = 8
HD = 128
HQ = 32


prior_weight = 0.5
norm_eps = 1e-05
key_block = 256


def per_device(
    step_embeds, step_len, leaf_of_step, cache_len, caches, norm_gain, qkv_weight, score_weight
):
    embeds = step_embeds[0]
    steps_here, seq_max, piece_width = embeds.shape
    row_width = norm_gain.shape[1]
    leaves_here = cache_len.shape[0]
    per_leaf = steps_here // leaves_here
    groups = caches.shape[3] // (2 * HD)
    group_size = HQ // KVH
    part_count = lax.axis_size("dp")
    dp_index = lax.axis_index("dp")
    per_peer = steps_here // part_count
    total_steps = leaf_of_step.shape[0]
    local_ids = jnp.arange(steps_here, dtype=jnp.int32)
    owners = (leaf_of_step // leaves_here).reshape(part_count, steps_here)
    send_orders = jnp.argsort(owners * steps_here + local_ids[None, :], axis=1)
    send_order = lax.dynamic_index_in_dim(send_orders, dp_index, 0, keepdims=False)
    sources = jnp.arange(part_count, dtype=jnp.int32)[:, None] * steps_here
    arriving = (
        lax.dynamic_slice_in_dim(send_orders, dp_index * per_peer, per_peer, 1) + sources
    ).reshape(steps_here)
    arrive_leaf = leaf_of_step[arriving] - dp_index * leaves_here
    arrange = jnp.argsort(arrive_leaf * total_steps + arriving)
    step_ids = arriving[arrange]
    lengths = step_len[step_ids].reshape(leaves_here, per_leaf)
    outgoing = embeds[send_order]
    local_rows = lax.all_gather(outgoing, "tensor", axis=2, tiled=True)
    as_float = local_rows.reshape(steps_here * seq_max, row_width).astype(jnp.float32)
    inverse_rms = lax.rsqrt(jnp.mean(as_float * as_float, axis=-1, keepdims=True) + norm_eps)
    normed = (as_float * inverse_rms * norm_gain[0]).astype(jnp.bfloat16)
    summed = jnp.dot(
        normed,
        lax.all_gather(qkv_weight[0], "dp", axis=0, tiled=True),
        preferred_element_type=jnp.float32,
    )
    outbound = summed.astype(jnp.bfloat16)
    outbound = outbound.reshape(part_count, per_peer, seq_max, outbound.shape[-1])
    arrived = lax.all_to_all(outbound, "dp", split_axis=0, concat_axis=0, tiled=True)
    projected = arrived.reshape(steps_here, seq_max, arrived.shape[-1])[arrange]
    projected = projected.reshape(leaves_here, per_leaf, seq_max, groups, group_size + 2, HD)
    queries = projected[:, :, :, :, :group_size]
    key_own = projected[:, :, :, :, group_size]
    value_own = projected[:, :, :, :, group_size + 1]
    scale_q = HD ** (-0.5)
    own_scores = (
        jnp.einsum("lsikgh,lsjkh->lsikgj", queries, key_own, preferred_element_type=jnp.float32)
        * scale_q
    )
    positions = jnp.arange(seq_max, dtype=jnp.int32)
    causal = positions[None, :] <= positions[:, None]
    own_scores = jnp.where(causal[:, None, None, :], own_scores, -jnp.inf)
    running_max = own_scores.max(-1)
    weights = jnp.exp(own_scores - running_max[..., None])
    running_sum = weights.sum(-1)
    weighted = jnp.einsum(
        "lsikgj,lsjkh->lsikgh",
        weights.astype(jnp.bfloat16),
        value_own,
        preferred_element_type=jnp.float32,
    )
    cache_rows = caches[0].reshape(leaves_here, caches.shape[2], groups, 2, HD)

    def visit(block_index, carry):
        old_max, old_sum, old_weighted = carry
        block_start = block_index * key_block
        block_rows = lax.dynamic_slice_in_dim(cache_rows, block_start, key_block, 1)
        block_keys = block_rows[:, :, :, 0]
        block_values = block_rows[:, :, :, 1]
        scores = (
            jnp.einsum(
                "lsikgh,lckh->lsikgc", queries, block_keys, preferred_element_type=jnp.float32
            )
            * scale_q
        )
        is_live = (block_start + jnp.arange(key_block, dtype=jnp.int32))[None, :] < cache_len[
            :, None
        ]
        scores = jnp.where(is_live[:, None, None, None, None, :], scores, -jnp.inf)
        new_max = jnp.maximum(old_max, scores.max(-1))
        rescale = jnp.exp(old_max - new_max)
        block_weights = jnp.exp(scores - new_max[..., None])
        new_sum = old_sum * rescale + block_weights.sum(-1)
        new_weighted = old_weighted * rescale[..., None] + jnp.einsum(
            "lsikgc,lckh->lsikgh",
            block_weights.astype(jnp.bfloat16),
            block_values,
            preferred_element_type=jnp.float32,
        )
        return (new_max, new_sum, new_weighted)

    block_count = cache_rows.shape[1] // key_block
    running_max, running_sum, weighted = lax.fori_loop(
        0, block_count, visit, (running_max, running_sum, weighted)
    )
    context = weighted / running_sum[..., None]
    is_valid = positions[None, None, :] < lengths[:, :, None]
    context = jnp.where(is_valid[:, :, :, None, None, None], context, 0.0)
    flat = context.reshape(leaves_here, per_leaf, seq_max, groups * group_size * HD)
    contexts = flat.astype(jnp.bfloat16)[None]
    last_token = (positions[None, None, :] == lengths[:, :, None] - 1).astype(jnp.float32)
    last_context = jnp.sum(last_token[:, :, :, None] * flat, axis=2)
    partial_value = jnp.sum(last_context * score_weight[0], axis=-1)
    model_weight = jnp.where(lax.axis_index("mp") == 0, prior_weight, 1.0).astype(jnp.float32)
    step_value = lax.psum(partial_value * model_weight, ("tensor", "mp"))
    return (contexts, step_value)


def solution(mesh):
    placed = (
        P("mp", "dp", None, "tensor"),
        P(),
        P(),
        P("dp"),
        P("mp", "dp", None, "tensor"),
        P("mp", None),
        P("mp", "dp", "tensor"),
        P("mp", "tensor"),
    )
    return jax.shard_map(
        per_device,
        mesh=mesh,
        in_specs=placed,
        out_specs=(P("mp", "dp", None, None, "tensor"), P("dp", None)),
        check_vma=False,
    )
```

profile of v0, /device:TPU:0, one launch (start us, length us, event | category | flops | bytes accessed | tf_op | source)
XLA Modules:
  0.0 1043.7 jit_solution(4711866427956556397)
XLA Ops:
  9.3 8.4 gather_fusion.3
  18.4 201.0 %all-gather.5.cloned.1.call-done = bf16[32,32,8192]{2,1,0:T(8,128)(2,1)} async-done(((bf16[32,32,4096]{2,1,0:T(8,128)(2,1)}), bf16[32,32,8192]{2,1,0:T(8,128)(2,1)}) %all-gather.5.cloned.1.call-update) | async-done | bytes 16777232 | tf_op jit(solution)/shard_map/all_gather | solution.py:43
  219.4 7.3 multiply_reduce_fusion
  226.7 17.3 %fusion.19 = bf16[1024,8192]{1,0:T(8,128)(2,1)} fusion(f32[8192]{0:T(1024)S(1)} %bitcast.129, f32[1024]{0:T(1024)S(1)} %rsqrt.12, bf16[32,32,8192]{2,1,0:T(8,128)(2,1)} %all-gather.5.cloned.1.call-done), kind=kLoop, calls=%fused_computation.32 | loop fusion | flops 33554432 | bytes 33591296 | tf_op jit(solution)/shard_map/convert_element_type | solution.py:46
  244.0 404.4 %all-gather.7.cloned.1.call-done = bf16[1,8192,3072]{2,1,0:T(8,128)(2,1)} async-done(((bf16[1,1024,3072]{2,1,0:T(8,128)(2,1)}), bf16[1,8192,3072]{2,1,0:T(8,128)(2,1)}) %all-gather.7.cloned.1.call-update) | async-done | bytes 50331664 | tf_op jit(solution)/shard_map/all_gather | solution.py:49
  648.5 62.0 %fusion.23 = bf16[1024,3072]{1,0:T(8,128)(2,1)} fusion(bf16[1024,8192]{1,0:T(8,128)(2,1)} %fusion.19, bf16[1,8192,3072]{2,1,0:T(8,128)(2,1)} %all-gather.7.cloned.1.call-done), kind=kOutput, calls=%fused_computation.41 | convolution fusion | flops 51542753280 | bytes 73400320 | tf_op jit(solution)/shard_map/dot_general | solution.py:47
  710.5 5.1 all-to-all-start
  716.4 8.6 copy.47
  728.3 126.1 %all-to-all-done = bf16[8,4,32,3072]{3,2,1,0:T(8,128)(2,1)} async-done(((bf16[8,4,32,3072]{3,2,1,0:T(8,128)(2,1)}), bf16[8,4,32,3072]{3,2,1,0:T(8,128)(2,1)}, u32[]{:S(2)}, u32[]{:S(2)}) %all-to-all-start) | async-done | bytes 6291488 | tf_op jit(solution)/shard_map/all_to_all | solution.py:54
  854.4 6.4 gather_fusion.4
  860.8 13.7 %reshape.183 = bf16[4,8,32,4,6,128]{5,4,3,2,1,0:T(8,128)(2,1)} reshape(bf16[32,32,3072]{2,1,0:T(8,128)(2,1)} %gather_fusion.4) | data formatting | bytes 12582912 | tf_op jit(solution)/shard_map/reshape | solution.py:56
  874.5 11.4 %fusion.45 = (bf16[4,8,32,4,1,128]{5,4,3,2,1,0:T(2,128)(2,1)}, bf16[4,8,32,4,1,128]{5,4,3,2,1,0:T(2,128)(2,1)}) fusion(bf16[4,8,32,4,6,128]{5,4,3,2,1,0:T(8,128)(2,1)} %reshape.183), kind=kLoop, calls=%fused_computation.84 | loop fusion | bytes 4194304 | tf_op jit(solution)/shard_map/slice | solution.py:59
  885.9 1.8 slice.37
  887.7 3.6 copy.52
  891.4 6.8 fusion.22
  898.3 3.0 fusion.21
  901.3 2.0 fusion.34
  903.3 4.3 copy.50
  907.7 100.4 %while.17 = (s32[]{:T(128)}, f32[4,8,32,4,4]{2,4,1,3,0:T(4,128)S(1)}, f32[4,8,32,4,4]{2,4,1,3,0:T(4,128)S(1)}, f32[4,8,32,4,4,128]{5,2,4,1,3,0:T(8,128)}, s32[4]...) while((s32[]{:T(128)}, ...), condition=%wide.region_8.9_spmd, body=%wide.region_5.8_spmd.sunk | while | flops 2197849344 | bytes 74455240 | solution.py:108
  907.8 10.6 %bitcast_reduce_fusion.2 = (f32[4,8,32,4,4]{2,4,1,3,0:T(4,128)S(1)}, f32[4,4,256,8,32,4]{2,4,5,3,1,0:T(8,128)}) fusion(pred[4,256]{1,0:T(4,128)(4,1)S(1)} %broadcast_compare_fusion.2, bf16[4,8,32,4,4,128]{5,2,4,1,3,0:T(8,128)(2,1)} %get-tuple-element.272, bf16[4,768,4,2,128]{1,4,3,2,0:T(8,128)(2,1)} %get-tuple-element.271, s32[]{:T(128)S(6)} %select_n.133), kind=kOutput, calls=%fused_computation.6.clone.1 | convolution fusion | flops 1086308352 | bytes 22086660 | tf_op jit(solution)/shard_map/while/body/eval_jaxpr/lsikgh,lckh->lsikgc/dot_general | solution.py:86
  918.5 8.8 fusion.53
  927.4 13.7 %bitcast_add_fusion.2 = f32[4,8,32,4,4,128]{5,2,4,1,3,0:T(8,128)} fusion(f32[4,8,32,4,4,128]{5,2,4,1,3,0:T(8,128)} %get-tuple-element.257, f32[4,8,32,4,4]{2,4,1,3,0:T(4,128)S(1)} %bitcast.123, f32[4,4,256,8,32,4]{2,4,5,3,1,0:T(8,128)} %get-tuple-element.239, f32[4,8,32,4,4]{2,4,1,3,0:T(4,128)S(1)} %max.8, ...), kind=kOutput, calls=%fused_computation.12.clone.1 | convolution fusion | flops 1094713344 | bytes 34735112 | tf_op jit(solution)/shard_map/while/body/eval_jaxpr/lsikgc,lckh->lsikgh/dot_general | solution.py:99
  941.3 10.6 %bitcast_reduce_fusion.2 = (f32[4,8,32,4,4]{2,4,1,3,0:T(4,128)S(1)}, f32[4,4,256,8,32,4]{2,4,5,3,1,0:T(8,128)}) fusion(pred[4,256]{1,0:T(4,128)(4,1)S(1)} %broadcast_compare_fusion.2, bf16[4,8,32,4,4,128]{5,2,4,1,3,0:T(8,128)(2,1)} %get-tuple-element.272, bf16[4,768,4,2,128]{1,4,3,2,0:T(8,128)(2,1)} %get-tuple-element.271, s32[]{:T(128)S(6)} %select_n.133), kind=kOutput, calls=%fused_computation.6.clone.1 | convolution fusion | flops 1086308352 | bytes 22086660 | tf_op jit(solution)/shard_map/while/body/eval_jaxpr/lsikgh,lckh->lsikgc/dot_general | solution.py:86
  952.0 8.8 fusion.53
  960.9 13.7 %bitcast_add_fusion.2 = f32[4,8,32,4,4,128]{5,2,4,1,3,0:T(8,128)} fusion(f32[4,8,32,4,4,128]{5,2,4,1,3,0:T(8,128)} %get-tuple-element.257, f32[4,8,32,4,4]{2,4,1,3,0:T(4,128)S(1)} %bitcast.123, f32[4,4,256,8,32,4]{2,4,5,3,1,0:T(8,128)} %get-tuple-element.239, f32[4,8,32,4,4]{2,4,1,3,0:T(4,128)S(1)} %max.8, ...), kind=kOutput, calls=%fused_computation.12.clone.1 | convolution fusion | flops 1094713344 | bytes 34735112 | tf_op jit(solution)/shard_map/while/body/eval_jaxpr/lsikgc,lckh->lsikgh/dot_general | solution.py:99
  974.7 10.6 %bitcast_reduce_fusion.2 = (f32[4,8,32,4,4]{2,4,1,3,0:T(4,128)S(1)}, f32[4,4,256,8,32,4]{2,4,5,3,1,0:T(8,128)}) fusion(pred[4,256]{1,0:T(4,128)(4,1)S(1)} %broadcast_compare_fusion.2, bf16[4,8,32,4,4,128]{5,2,4,1,3,0:T(8,128)(2,1)} %get-tuple-element.272, bf16[4,768,4,2,128]{1,4,3,2,0:T(8,128)(2,1)} %get-tuple-element.271, s32[]{:T(128)S(6)} %select_n.133), kind=kOutput, calls=%fused_computation.6.clone.1 | convolution fusion | flops 1086308352 | bytes 22086660 | tf_op jit(solution)/shard_map/while/body/eval_jaxpr/lsikgh,lckh->lsikgc/dot_general | solution.py:86
  985.4 8.8 fusion.53
  994.4 13.7 %bitcast_add_fusion.2 = f32[4,8,32,4,4,128]{5,2,4,1,3,0:T(8,128)} fusion(f32[4,8,32,4,4,128]{5,2,4,1,3,0:T(8,128)} %get-tuple-element.257, f32[4,8,32,4,4]{2,4,1,3,0:T(4,128)S(1)} %bitcast.123, f32[4,4,256,8,32,4]{2,4,5,3,1,0:T(8,128)} %get-tuple-element.239, f32[4,8,32,4,4]{2,4,1,3,0:T(4,128)S(1)} %max.8, ...), kind=kOutput, calls=%fused_computation.12.clone.1 | convolution fusion | flops 1094713344 | bytes 34735112 | tf_op jit(solution)/shard_map/while/body/eval_jaxpr/lsikgc,lckh->lsikgh/dot_general | solution.py:99
  1008.1 6.2 multiply_reduce_fusion.1
  1014.4 4.1 copy.53
  1018.4 7.8 convert_element_type.52
  1026.4 10.4 %psum.7 = f32[4,8]{1,0:T(4,128)} all-reduce(f32[4,8]{1,0:T(4,128)S(1)} %broadcast_multiply_fusion), channel_id=1, replica_groups=mesh['dp'=8,'tensor'=2,'mp'=2] {'tensor','mp'}, use_global_device_ids=true, to_apply=%region_11.12 | all-reduce | flops 32 | bytes 256 | tf_op jit(solution)/shard_map/psum | solution.py:120
  (73 shorter events, 8.5 us)
Async XLA Ops:
  7.2 720.2 %copy-start = (s32[256]{0:T(256)S(1)}, s32[256]{0:T(256)}, u32[]{:S(2)}) copy-start(s32[256]{0:T(256)} %param.11) | copy-start | bytes 3076
  7.2 212.2 %all-gather.5.cloned.1.call-start = ((), (), s32[]{:S(2)}) async-start(), calls=%async_computation.1 | async-start | bytes 25165824 | tf_op jit(solution)/shard_map/all_gather | solution.py:43
  17.7 630.8 %all-gather.7.cloned.1.call-start = ((), (), s32[]{:S(2)}) async-start(), calls=%async_computation.2 | async-start | bytes 56623104 | tf_op jit(solution)/shard_map/all_gather | solution.py:49
  18.4 208.3 %copy-start.6 = (f32[1,8192]{1,0:T(1,128)S(1)}, f32[1,8192]{1,0:T(1,128)}, u32[]{:S(2)}) copy-start(f32[1,8192]{1,0:T(1,128)} %param.15) | copy-start | bytes 98308
  710.5 5.2 copy-start.2
  710.5 143.8 %all-to-all-start = ((bf16[8,4,32,3072]{3,2,1,0:T(8,128)(2,1)}), bf16[8,4,32,3072]{3,2,1,0:T(8,128)(2,1)}, u32[]{:S(2)}, u32[]{:S(2)}) async-start(bf16[8,4,32,3072]{3,2,1,0:T(8,128)(2,1)} %bitcast.128), calls=%async_computation | async-start | bytes 12582912 | tf_op jit(solution)/shard_map/all_to_all | solution.py:54
  874.5 11.4 %copy-start.3 = (bf16[4,8,32,4,6,128]{5,4,3,2,1,0:T(8,128)(2,1)S(1)}, bf16[4,8,32,4,6,128]{5,4,3,2,1,0:T(8,128)(2,1)}, u32[]{:S(2)}) copy-start(bf16[4,8,32,4,6,128]{5,4,3,2,1,0:T(8,128)(2,1)} %reshape.183) | copy-start | bytes 18874372
  887.7 3.6 copy-start.5
  891.4 9.9 copy-start.4
  903.3 4.4 copy-start.7
  1014.3 22.5 %copy-start.1 = (s32[256]{0:T(256)S(1)}, s32[256]{0:T(256)}, u32[]{:S(2)}) copy-start(s32[256]{0:T(256)} %param.11) | copy-start | bytes 3076
  1014.3 11.9 %copy-start.8 = (f32[1,2048]{1,0:T(1,128)S(1)}, f32[1,2048]{1,0:T(1,128)}, u32[]{:S(2)}) copy-start(f32[1,2048]{1,0:T(1,128)} %param.17) | copy-start | bytes 24580
Sparse Core Ops, SparseCore 0:
  17.8 201.5 all-gather.4
  221.0 427.3 all-gather.6
where the time goes:
time: 1040 us
  waiting for transfers between devices  732 us (70%)
  matrix products  144 us (14%)
  local copies, waits for them, and re-layouts  73.2 us (7%)
  other arithmetic  64.6 us (6%)
  between operations  14.2 us (1%)
  blocking collectives  10.4 us (1%)
    all_gather x1, waiting for transfers between devices, per_device(): lax.all_gather(qkv_weight[0], 'dp', axis=0, tiled=True)  404 us
    all_gather x1, waiting for transfers between devices, per_device(): local_rows = lax.all_gather(outgoing, 'tensor', axis=2, tiled=True)  201 us
    all_to_all x1, waiting for transfers between devices, per_device(): lax.all_to_all(outbound, 'dp', split_axis=0, concat_axis=0, tiled=True)  126 us
    dot_general x1, matrix products, per_device(): jnp.dot(normed, lax.all_gather(qkv_weight[0], 'dp', axis=0, tiled=True),...  62 us
    dot_general x3, matrix products, visit(): jnp.einsum('lsikgc,lckh->lsikgh', block_weights.astype(jnp.bfloat16), blo...  41 us
    dot_general x3, matrix products, visit(): jnp.einsum('lsikgh,lckh->lsikgc', queries, block_keys, preferred_element_...  31.9 us
    reduce_sum x3, other arithmetic, visit(): new_sum = old_sum * rescale + block_weights.sum(-1)  26.3 us
  transfers between devices with their start and end apart: 3, of which 3 were waited for; matrix products, arithmetic and copies ran while one was open for 4% of the time, Pallas kernels for 0%

commit v1 on v0

v1 whole, which is shorter than its diff:
```python
import functools

import jax
import jax.numpy as jnp
from jax import lax
from jax.experimental import pallas as pl
from jax.experimental.pallas import tpu as pltpu
from jax.sharding import PartitionSpec as P

KVH = 8
HD = 128
HQ = 32


prior_weight = 0.5
norm_eps = 1e-05


def permute_kernel(order_ref, rows_ref, out_ref):
    def move(slot, carry):
        out_ref[slot] = rows_ref[order_ref[slot]]
        return carry

    lax.fori_loop(0, out_ref.shape[0], move, 0)


def permute_steps(order, rows):
    size = rows.size * rows.dtype.itemsize
    return pl.pallas_call(
        permute_kernel,
        out_shape=jax.ShapeDtypeStruct(rows.shape, rows.dtype),
        in_specs=[
            pl.BlockSpec(memory_space=pltpu.SMEM),
            pl.BlockSpec(memory_space=pltpu.VMEM),
        ],
        out_specs=pl.BlockSpec(memory_space=pltpu.VMEM),
        compiler_params=pltpu.CompilerParams(vmem_limit_bytes=2 * size + (4 << 20)),
        cost_estimate=pl.CostEstimate(flops=0, bytes_accessed=2 * size, transcendentals=0),
    )(order, rows)


def attend_kernel(
    per_leaf,
    group_size,
    arrange_ref,
    length_ref,
    live_ref,
    rows_ref,
    cache_ref,
    weight_ref,
    *refs,
):
    out_ref, score_ref, query_s, key_s, value_s = refs[-5:]
    leaf = pl.program_id(0)
    seq_max = rows_ref.shape[1]
    cache_rows = cache_ref.shape[2]
    steps_tile = query_s.shape[1] // seq_max
    tile = steps_tile * seq_max
    keys = cache_rows + tile
    key_s[:cache_rows] = cache_ref[0, 0, :, :HD]
    value_s[:cache_rows] = cache_ref[0, 0, :, HD:]
    row = lax.broadcasted_iota(jnp.int32, (tile, keys), 0)
    column = lax.broadcasted_iota(jnp.int32, (tile, keys), 1)
    own = column - cache_rows
    first = row - lax.rem(row, seq_max)
    far_ok = column < jnp.minimum(live_ref[leaf], cache_rows)
    own_ok = (own >= first) & (own <= row)
    bias = jnp.where(far_ok | own_ok, 0.0, -jnp.inf)
    token = lax.broadcasted_iota(jnp.int32, (seq_max, HD), 0)
    scale_q = HD ** (-0.5)
    for part in range(per_leaf // steps_tile):
        valid, last = [], []
        for place in range(steps_tile):
            slot = leaf * per_leaf + part * steps_tile + place
            step = arrange_ref[slot]
            span = pl.ds(place * seq_max, seq_max)
            for head in range(group_size):
                query_s[head, span] = rows_ref[step, :, head * HD : (head + 1) * HD]
            key_s[pl.ds(cache_rows + place * seq_max, seq_max)] = rows_ref[
                step, :, group_size * HD : (group_size + 1) * HD
            ]
            value_s[pl.ds(cache_rows + place * seq_max, seq_max)] = rows_ref[
                step, :, (group_size + 1) * HD : (group_size + 2) * HD
            ]
            valid.append(token < length_ref[slot])
            last.append((token == length_ref[slot] - 1).astype(jnp.float32))
        step_score = [jnp.zeros((1, HD), jnp.float32) for _ in range(steps_tile)]
        for head in range(group_size):
            scores = lax.dot_general(
                query_s[head],
                key_s[...],
                (((1,), (1,)), ((), ())),
                preferred_element_type=jnp.float32,
            )
            scores = scores * scale_q + bias
            probs = jnp.exp(scores - scores.max(-1, keepdims=True))
            total = probs.sum(-1, keepdims=True)
            context = jnp.dot(
                probs.astype(jnp.bfloat16), value_s[...], preferred_element_type=jnp.float32
            )
            context = context / total
            for place in range(steps_tile):
                piece = jnp.where(
                    valid[place], context[place * seq_max : (place + 1) * seq_max], 0.0
                )
                out_ref[0, 0, part * steps_tile + place, :, head * HD : (head + 1) * HD] = (
                    piece.astype(jnp.bfloat16)
                )
                step_score[place] += (piece * last[place]).sum(0, keepdims=True) * weight_ref[
                    :, head * HD : (head + 1) * HD
                ]
        for place in range(steps_tile):
            score_ref[0, pl.ds(part * steps_tile + place, 1)] = step_score[place]


def attend(group, groups, per_leaf, arrange, lengths, live, rows, caches, weight, contexts):
    steps_here, seq_max, columns = rows.shape
    _, leaves_here, cache_rows, _ = caches.shape
    group_size = HQ // KVH
    tile = 128
    width = group_size * HD
    in_specs = [
        pl.BlockSpec((steps_here, seq_max, columns), lambda l, *_: (0, 0, 0)),
        pl.BlockSpec((1, 1, cache_rows, 2 * HD), lambda l, *_: (0, l, 0, group)),
        pl.BlockSpec((1, width), lambda l, *_: (0, group)),
    ]
    operands = [rows, caches, weight]
    aliases = {}
    if contexts is not None:
        in_specs.append(pl.BlockSpec(memory_space=pl.ANY))
        operands.append(contexts)
        aliases = {6: 0}
    work = steps_here * seq_max * group_size * (cache_rows + tile)
    return pl.pallas_call(
        functools.partial(attend_kernel, per_leaf, group_size),
        grid_spec=pltpu.PrefetchScalarGridSpec(
            num_scalar_prefetch=3,
            grid=(leaves_here,),
            in_specs=in_specs,
            out_specs=[
                pl.BlockSpec(
                    (1, 1, per_leaf, seq_max, width), lambda l, *_: (0, l, 0, 0, group)
                ),
                pl.BlockSpec((1, per_leaf, HD), lambda l, *_: (l, 0, 0)),
            ],
            scratch_shapes=[
                pltpu.VMEM((group_size, tile, HD), jnp.bfloat16),
                pltpu.VMEM((cache_rows + tile, HD), jnp.bfloat16),
                pltpu.VMEM((cache_rows + tile, HD), jnp.bfloat16),
            ],
        ),
        out_shape=[
            jax.ShapeDtypeStruct(
                (1, leaves_here, per_leaf, seq_max, groups * width), jnp.bfloat16
            ),
            jax.ShapeDtypeStruct((leaves_here, per_leaf, HD), jnp.float32),
        ],
        input_output_aliases=aliases,
        compiler_params=pltpu.CompilerParams(vmem_limit_bytes=24 << 20),
        cost_estimate=pl.CostEstimate(
            flops=4 * work * HD, bytes_accessed=8 << 20, transcendentals=work
        ),
    )(arrange, lengths, live, *operands)


def per_device(
    step_embeds, step_len, leaf_of_step, cache_len, caches, norm_gain, qkv_weight, score_weight
):
    embeds = step_embeds[0]
    steps_here, seq_max, piece_width = embeds.shape
    row_width = norm_gain.shape[1]
    leaves_here = cache_len.shape[0]
    per_leaf = steps_here // leaves_here
    groups = caches.shape[3] // (2 * HD)
    group_size = HQ // KVH
    part_count = lax.axis_size("dp")
    dp_index = lax.axis_index("dp")
    tensor_count = lax.axis_size("tensor")
    tensor_index = lax.axis_index("tensor")
    per_peer = steps_here // part_count
    total_steps = leaf_of_step.shape[0]

    own = embeds.reshape(steps_here * seq_max, piece_width)
    width = (group_size + 2) * HD
    gathered = [
        lax.all_gather(
            qkv_weight[0, :, g * width : (g + 1) * width], "dp", axis=0, tiled=True
        )
        for g in range(groups)
    ]
    local_rows = jnp.zeros((steps_here * seq_max, row_width), own.dtype)
    for shift in range(tensor_count):
        source = lax.rem(tensor_index + tensor_count - shift, tensor_count)
        piece = own
        if shift:
            hops = [(i, (i + shift) % tensor_count) for i in range(tensor_count)]
            piece = lax.ppermute(own, "tensor", hops)
        local_rows = lax.dynamic_update_slice_in_dim(
            local_rows, piece, source * piece_width, 1
        )

    local_ids = jnp.arange(steps_here, dtype=jnp.int32)
    owners = (leaf_of_step // leaves_here).reshape(part_count, steps_here)
    send_orders = jnp.argsort(owners * steps_here + local_ids[None, :], axis=1)
    send_order = lax.dynamic_index_in_dim(send_orders, dp_index, 0, keepdims=False)
    sources = jnp.arange(part_count, dtype=jnp.int32)[:, None] * steps_here
    arriving = (
        lax.dynamic_slice_in_dim(send_orders, dp_index * per_peer, per_peer, 1) + sources
    ).reshape(steps_here)
    arrive_leaf = leaf_of_step[arriving] - dp_index * leaves_here
    arrange = jnp.argsort(arrive_leaf * total_steps + arriving).astype(jnp.int32)
    lengths = step_len[arriving[arrange]]

    as_float = local_rows.astype(jnp.float32)
    inverse_rms = lax.rsqrt(jnp.mean(as_float * as_float, axis=-1, keepdims=True) + norm_eps)
    normed = (as_float * inverse_rms * norm_gain[0]).astype(jnp.bfloat16)

    contexts, partial_value = None, 0.0
    for g in range(groups):
        summed = jnp.dot(normed, gathered[g], preferred_element_type=jnp.float32)
        outbound = summed.astype(jnp.bfloat16).reshape(steps_here, seq_max, width)
        outbound = permute_steps(send_order, outbound)
        outbound = outbound.reshape(part_count, per_peer, seq_max, width)
        arrived = lax.all_to_all(outbound, "dp", split_axis=0, concat_axis=0, tiled=True)
        arrived = arrived.reshape(steps_here, seq_max, width)
        contexts, shares = attend(
            g, groups, per_leaf, arrange, lengths, cache_len, arrived, caches, score_weight, contexts
        )
        partial_value = partial_value + jnp.sum(shares, axis=-1)
    model_weight = jnp.where(lax.axis_index("mp") == 0, prior_weight, 1.0).astype(jnp.float32)
    step_value = lax.psum(partial_value * model_weight, ("tensor", "mp"))
    return (contexts, step_value)


def solution(mesh):
    placed = (
        P("mp", "dp", None, "tensor"),
        P(),
        P(),
        P("dp"),
        P("mp", "dp", None, "tensor"),
        P("mp", None),
        P("mp", "dp", "tensor"),
        P("mp", "tensor"),
    )
    return jax.shard_map(
        per_device,
        mesh=mesh,
        in_specs=placed,
        out_specs=(P("mp", "dp", None, None, "tensor"), P("dp", None)),
        check_vma=False,
    )
```

time: 1040 us -> 682 us (0.66)
  waiting for transfers between devices: 732 us -> 441 us
  Pallas kernels: 0 us -> 64.6 us
  matrix products: 144 us -> 79.7 us
  other arithmetic: 64.6 us -> 10.8 us
  local copies, waits for them, and re-layouts: 73.2 us -> 39.9 us
  starting transfers between devices: 5.14 us -> 20.4 us
    all_gather x2 -> x4, waiting for transfers between devices: 605 us -> 246 us  [per_device(): lax.all_gather(qkv_weight[0, :, g * width:(g + 1) * width], 'dp', axis=0,...]
    ppermute x0 -> x1, waiting for transfers between devices: none -> 164 us  [per_device(): piece = lax.ppermute(own, 'tensor', hops)]
    all_to_all x1 -> x4, waiting for transfers between devices: 126 us -> 30.1 us  [per_device(): lax.all_to_all(outbound, 'dp', split_axis=0, concat_axis=0, tiled=True)]
    pallas_call x0 -> x8, Pallas kernels: none -> 64.6 us  [the longest x4 56.7 us: attend(): pl.pallas_call(functools.partial(attend_kernel, per_leaf, group_size), gr...]
    dot_general x9 -> x4, matrix products: 144 us -> 79.7 us  [per_device(): summed = jnp.dot(normed, gathered[g], preferred_element_type=jnp.float32)]
    reduce_sum x6 -> x4, other arithmetic: 35.6 us -> 0.34 us  [per_device(): partial_value = partial_value + jnp.sum(shares, axis=-1)]
    convert_element_type x2 -> x0, other arithmetic: 17.4 us -> none  [the longest x1 17.3 us: per_device(): normed = (as_float * inverse_rms * norm_gain[0]).astype(jnp.bfloat16)]
    dynamic_update_slice x0 -> x2, local copies, waits for them, and re-layouts: none -> 16.5 us  [per_device(): lax.dynamic_update_slice_in_dim(local_rows, piece, source * piece_width, 1)]
  transfers between devices with their start and end apart: 3 -> 9, of which waited for: 3 -> 5; matrix products, arithmetic and copies ran while one was open for 4% -> 17% of each run, Pallas kernels for 0% -> 7%
where the time goes in v1:
time: 682 us; the launch traced here: 681 us
  waiting for transfers between devices  441 us (65%)
  matrix products  79.7 us (12%)
  Pallas kernels  64.6 us (9%)
  local copies, waits for them, and re-layouts  39.9 us (6%)
  starting transfers between devices  20.4 us (3%)
  between operations  14 us (2%)
  other arithmetic  10.8 us (2%)
  blocking collectives  10.4 us (2%)
    all_gather x4, waiting for transfers between devices, per_device(): lax.all_gather(qkv_weight[0, :, g * width:(g + 1) * width], 'dp', axis=0,...  246 us
    ppermute x1, waiting for transfers between devices, per_device(): piece = lax.ppermute(own, 'tensor', hops)  164 us
    dot_general x4, matrix products, per_device(): summed = jnp.dot(normed, gathered[g], preferred_element_type=jnp.float32)  79.7 us
    pallas_call x4, Pallas kernels, attend(): pl.pallas_call(functools.partial(attend_kernel, per_leaf, group_size), gr...  56.7 us
    all_to_all x4, waiting for transfers between devices, per_device(): lax.all_to_all(outbound, 'dp', split_axis=0, concat_axis=0, tiled=True)  30.1 us
    all_to_all x4, starting transfers between devices, per_device(): lax.all_to_all(outbound, 'dp', split_axis=0, concat_axis=0, tiled=True)  17.2 us
    dynamic_update_slice x2, local copies, waits for them, and re-layouts, per_device(): lax.dynamic_update_slice_in_dim(local_rows, piece, source * piece_width, 1)  16.5 us
  transfers between devices with their start and end apart: 9, of which 5 were waited for; matrix products, arithmetic and copies ran while one was open for 17% of the time, Pallas kernels for 7%

profile of v1, /device:TPU:0, one launch (start us, length us, event | category | flops | bytes accessed | tf_op | source)
XLA Modules:
  0.0 681.0 jit_solution(7578520502661016865)
XLA Ops:
  7.2 5.7 fusion.30
  14.5 3.0 collective-permute-start
  18.8 6.6 broadcast_in_dim.5
  25.3 8.6 %constant_dynamic-update-slice_fusion.1 = bf16[1024,8192]{1,0:T(8,128)(2,1)} fusion(bf16[1024,8192]{1,0:T(8,128)(2,1)} %broadcast_in_dim.5, bf16[1024,4096]{1,0:T(8,128)(2,1)} %bitcast.47, s32[]{:T(128)S(6)} %select_n.51), kind=kLoop, calls=%fused_computation.36 | loop fusion | bytes 16777220 | tf_op jit(solution)/shard_map/dynamic_update_slice | solution.py:198
  34.0 164.4 %collective-permute-done = bf16[1024,4096]{1,0:T(8,128)(2,1)} collective-permute-done((bf16[1024,4096]{1,0:T(8,128)(2,1)}, bf16[1024,4096]{1,0:T(8,128)(2,1)}, u32[]{:S(2)}, u32[]{:S(2)}) %collective-permute-start) | collective-permute-done | bytes 8388640 | tf_op jit(solution)/shard_map/ppermute | solution.py:197
  198.3 7.8 %constant_dynamic-update-slice_fusion = bf16[1024,8192]{1,0:T(8,128)(2,1)} fusion(bf16[1024,8192]{1,0:T(8,128)(2,1)} %constant_dynamic-update-slice_fusion.1, bf16[1024,4096]{1,0:T(8,128)(2,1)} %collective-permute-done, s32[]{:T(128)S(6)} %select_n.52), kind=kLoop, calls=%fused_computation.35 | loop fusion | bytes 16777220 | tf_op jit(solution)/shard_map/dynamic_update_slice | solution.py:198
  206.2 7.3 %fusion = f32[1024]{0:T(1024)S(1)} fusion(bf16[1024,8192]{1,0:T(8,128)(2,1)} %constant_dynamic-update-slice_fusion), kind=kLoop, calls=%fused_computation.5 | loop fusion | flops 25164800 | bytes 16781312 | tf_op jit(solution)/shard_map/reduce_sum | solution.py:215
  213.5 20.1 %fusion.20 = bf16[1024,768]{1,0:T(8,128)(2,1)S(1)} fusion(bf16[1,8192,768]{2,1,0:T(8,128)(2,1)} %all-gather.15.cloned.1.call-done, bf16[1024,8192]{1,0:T(8,128)(2,1)} %constant_dynamic-update-slice_fusion, f32[8192]{0:T(1024)S(1)} %bitcast.48, f32[1024]{0:T(1024)S(1)} %add_rsqrt_fusion), kind=kOutput, calls=%fused_computation.19 | convolution fusion | flops 12919242752 | bytes 30969856 | tf_op jit(solution)/shard_map/dot_general | solution.py:220
  233.6 2.0 shard_map.98
  235.5 4.8 all-to-all-start.3
  240.4 14.3 %all-gather.13.cloned.1.call-done = bf16[1,8192,768]{2,1,0:T(8,128)(2,1)} async-done(((bf16[1,1024,768]{2,1,0:T(8,128)(2,1)}), bf16[1,8192,768]{2,1,0:T(8,128)(2,1)}) %all-gather.13.cloned.1.call-update) | async-done | bytes 12582928 | tf_op jit(solution)/shard_map/all_gather | solution.py:186
  254.7 19.9 %fusion.17 = bf16[1024,768]{1,0:T(8,128)(2,1)S(1)} fusion(bf16[1,8192,768]{2,1,0:T(8,128)(2,1)} %all-gather.13.cloned.1.call-done, bf16[1024,8192]{1,0:T(8,128)(2,1)} %constant_dynamic-update-slice_fusion, f32[8192]{0:T(1024)S(1)} %bitcast.49, f32[1024]{0:T(1024)S(1)} %add_rsqrt_fusion), kind=kOutput, calls=%fused_computation.18 | convolution fusion | flops 12919242752 | bytes 30969856 | tf_op jit(solution)/shard_map/dot_general | solution.py:220
  274.5 2.0 shard_map.97
  276.5 30.1 %all-to-all-done.3 = bf16[8,4,32,768]{3,2,1,0:T(8,128)(2,1)S(1)} async-done(((bf16[8,4,32,768]{3,2,1,0:T(8,128)(2,1)}), bf16[8,4,32,768]{3,2,1,0:T(8,128)(2,1)S(1)}, u32[]{:S(2)}, u32[]{:S(2)}) %all-to-all-start.3) | async-done | bytes 1572896 | tf_op jit(solution)/shard_map/all_to_all | solution.py:224
  306.6 3.6 all-to-all-start.2
  310.2 107.7 %all-gather.11.cloned.1.call-done = bf16[1,8192,768]{2,1,0:T(8,128)(2,1)} async-done(((bf16[1,1024,768]{2,1,0:T(8,128)(2,1)}), bf16[1,8192,768]{2,1,0:T(8,128)(2,1)}) %all-gather.11.cloned.1.call-update) | async-done | bytes 12582928 | tf_op jit(solution)/shard_map/all_gather | solution.py:186
  417.9 19.9 %fusion.14 = bf16[1024,768]{1,0:T(8,128)(2,1)S(1)} fusion(bf16[1,8192,768]{2,1,0:T(8,128)(2,1)} %all-gather.11.cloned.1.call-done, bf16[1024,8192]{1,0:T(8,128)(2,1)} %constant_dynamic-update-slice_fusion, f32[8192]{0:T(1024)S(1)} %bitcast.50, f32[1024]{0:T(1024)S(1)} %add_rsqrt_fusion), kind=kOutput, calls=%fused_computation.17 | convolution fusion | flops 12919242752 | bytes 30969856 | tf_op jit(solution)/shard_map/dot_general | solution.py:220
  437.7 2.0 shard_map.96
  439.7 4.5 all-to-all-start.1
  444.2 123.5 %all-gather.9.cloned.1.call-done = bf16[1,8192,768]{2,1,0:T(8,128)(2,1)} async-done(((bf16[1,1024,768]{2,1,0:T(8,128)(2,1)}), bf16[1,8192,768]{2,1,0:T(8,128)(2,1)}) %all-gather.9.cloned.1.call-update) | async-done | bytes 12582928 | tf_op jit(solution)/shard_map/all_gather | solution.py:186
  567.7 19.9 %fusion.11 = bf16[1024,768]{1,0:T(8,128)(2,1)S(1)} fusion(bf16[1,8192,768]{2,1,0:T(8,128)(2,1)} %all-gather.9.cloned.1.call-done, bf16[1024,8192]{1,0:T(8,128)(2,1)} %constant_dynamic-update-slice_fusion, f32[8192]{0:T(1024)S(1)} %bitcast.51, f32[1024]{0:T(1024)S(1)} %add_rsqrt_fusion), kind=kOutput, calls=%fused_computation.16 | convolution fusion | flops 12919242752 | bytes 30969856 | tf_op jit(solution)/shard_map/dot_general | solution.py:220
  587.6 2.0 shard_map.95
  589.6 4.3 all-to-all-start
  595.6 1.6 sort.35
  598.6 2.8 copy-done.1
  601.4 13.5 %shard_map.99 = (bf16[1,4,8,32,2048]{4,3,2,1,0:T(8,128)(2,1)}, f32[4,8,128]{2,1,0:T(8,128)S(1)}) custom-call(s32[32]{0:T(128)S(1)} %get-tuple-element.13.arrange_ref, s32[32]{0:T(128)S(1)} %gather_fusion.2, s32[4]{0:T(128)S(1)} %copy-done.5, bf16[32,32,768]{2,1,0:T(8,128)(2,1)S(1)} %bitcast.40, bf16[1,4,768,1024]{3,2,1,0:T(8,128)(2,1)S(1)} %copy-done.1, ...), custom_call_target="tpu_custom_call" | custom-call | flops 1879048192 | bytes 8388608 | tf_op jit(solution)/shard_map/pallas_call | solution.py:134
  614.9 2.8 copy-done.2
  617.7 13.5 %shard_map.100 = (bf16[1,4,8,32,2048]{4,3,2,1,0:T(8,128)(2,1)}, f32[4,8,128]{2,1,0:T(8,128)S(1)}) custom-call(s32[32]{0:T(128)S(1)} %get-tuple-element.13.arrange_ref, s32[32]{0:T(128)S(1)} %gather_fusion.2, s32[4]{0:T(128)S(1)} %copy-done.5, bf16[32,32,768]{2,1,0:T(8,128)(2,1)S(1)} %bitcast.41, ...), custom_call_target="tpu_custom_call", output_to_operand_aliasing={{0}: (6, {})} | custom-call | flops 1879048192 | bytes 8388608 | tf_op jit(solution)/shard_map/pallas_call | solution.py:134
  631.2 14.9 %shard_map.101 = (bf16[1,4,8,32,2048]{4,3,2,1,0:T(8,128)(2,1)}, f32[4,8,128]{2,1,0:T(8,128)S(1)}) custom-call(s32[32]{0:T(128)S(1)} %get-tuple-element.13.arrange_ref, s32[32]{0:T(128)S(1)} %gather_fusion.2, s32[4]{0:T(128)S(1)} %copy-done.5, bf16[32,32,768]{2,1,0:T(8,128)(2,1)} %bitcast.12.rows_ref, ...), custom_call_target="tpu_custom_call", output_to_operand_aliasing={{0}: (6, {})} | custom-call | flops 1879048192 | bytes 8388608 | tf_op jit(solution)/shard_map/pallas_call | solution.py:134
  646.1 2.8 copy-done.3
  648.9 14.9 %shard_map.102 = (bf16[1,4,8,32,2048]{4,3,2,1,0:T(8,128)(2,1)}, f32[4,8,128]{2,1,0:T(8,128)S(1)}) custom-call(s32[32]{0:T(128)S(1)} %get-tuple-element.13.arrange_ref, s32[32]{0:T(128)S(1)} %gather_fusion.2, s32[4]{0:T(128)S(1)} %copy-done.5, bf16[32,32,768]{2,1,0:T(8,128)(2,1)} %bitcast.8.rows_ref, ...), custom_call_target="tpu_custom_call", output_to_operand_aliasing={{0}: (6, {})} | custom-call | flops 1879048192 | bytes 8388608 | tf_op jit(solution)/shard_map/pallas_call | solution.py:134
  664.1 10.4 %psum.7 = f32[4,8]{1,0:T(4,128)} all-reduce(f32[4,8]{1,0:T(4,128)S(1)} %add_multiply_fusion), channel_id=1, replica_groups=mesh['dp'=8,'tensor'=2,'mp'=2] {'tensor','mp'}, use_global_device_ids=true, to_apply=%region_7.8 | all-reduce | flops 32 | bytes 256 | tf_op jit(solution)/shard_map/psum | solution.py:231
  (58 shorter events, 6.3 us)
Async XLA Ops:
  7.2 590.7 %copy-start = (s32[256]{0:T(256)S(1)}, s32[256]{0:T(256)}, u32[]{:S(2)}) copy-start(s32[256]{0:T(256)} %param.9) | copy-start | bytes 3076
  7.2 10.4 %copy-start.6 = (s32[256]{0:T(256)S(1)}, s32[256]{0:T(256)}, u32[]{:S(2)}) copy-start(s32[256]{0:T(256)} %param.10) | copy-start | bytes 3076
  7.2 206.3 %all-gather.15.cloned.1.call-start = ((), (), s32[]{:S(2)}) async-start(), calls=%async_computation.7 | async-start | bytes 14155776 | tf_op jit(solution)/shard_map/all_gather | solution.py:186
  13.0 241.7 %all-gather.13.cloned.1.call-start = ((), (), s32[]{:S(2)}) async-start(), calls=%async_computation.6 | async-start | bytes 14155776 | tf_op jit(solution)/shard_map/all_gather | solution.py:186
  13.7 404.1 %all-gather.11.cloned.1.call-start = ((), (), s32[]{:S(2)}) async-start(), calls=%async_computation.5 | async-start | bytes 14155776 | tf_op jit(solution)/shard_map/all_gather | solution.py:186
  14.5 553.3 %all-gather.9.cloned.1.call-start = ((), (), s32[]{:S(2)}) async-start(), calls=%async_computation.4 | async-start | bytes 14155776 | tf_op jit(solution)/shard_map/all_gather | solution.py:186
  14.5 183.8 %collective-permute-start = (bf16[1024,4096]{1,0:T(8,128)(2,1)}, bf16[1024,4096]{1,0:T(8,128)(2,1)}, u32[]{:S(2)}, u32[]{:S(2)}) collective-permute-start(bf16[1024,4096]{1,0:T(8,128)(2,1)} %bitcast.46), channel_id=1, source_target_pairs={{0,2},{2,0},{1,3},{3,1},{4,6},{6,4},{5,7},{7,5},{8,10},{10,8},{9,1... | collective-permute-start | bytes 25165832 | tf_op jit(solution)/shard_map/ppermute | solution.py:197
  18.6 15.4 %copy-start.8 = (s32[8,32]{0,1:T(8,128)}, s32[8,32]{0,1:T(8,128)S(1)}, u32[]{:S(2)}) copy-start(s32[8,32]{0,1:T(8,128)S(1)} %get-tuple-element.12) | copy-start | bytes 3076
  206.2 7.3 %copy-start.9 = (f32[1,8192]{1,0:T(1,128)S(1)}, f32[1,8192]{1,0:T(1,128)}, u32[]{:S(2)}) copy-start(f32[1,8192]{1,0:T(1,128)} %param.13) | copy-start | bytes 98308
  235.5 71.0 %all-to-all-start.3 = ((bf16[8,4,32,768]{3,2,1,0:T(8,128)(2,1)}), bf16[8,4,32,768]{3,2,1,0:T(8,128)(2,1)S(1)}, u32[]{:S(2)}, u32[]{:S(2)}) async-start(bf16[8,4,32,768]{3,2,1,0:T(8,128)(2,1)} %bitcast.19), calls=%async_computation.3 | async-start | bytes 3145728 | tf_op jit(solution)/shard_map/all_to_all | solution.py:224
  306.6 133.1 %all-to-all-start.2 = ((bf16[8,4,32,768]{3,2,1,0:T(8,128)(2,1)}), bf16[8,4,32,768]{3,2,1,0:T(8,128)(2,1)S(1)}, u32[]{:S(2)}, u32[]{:S(2)}) async-start(bf16[8,4,32,768]{3,2,1,0:T(8,128)(2,1)} %bitcast.15), calls=%async_computation.2 | async-start | bytes 3145728 | tf_op jit(solution)/shard_map/all_to_all | solution.py:224
  439.7 149.9 %all-to-all-start.1 = ((bf16[8,4,32,768]{3,2,1,0:T(8,128)(2,1)}), bf16[8,4,32,768]{3,2,1,0:T(8,128)(2,1)}, u32[]{:S(2)}, u32[]{:S(2)}) async-start(bf16[8,4,32,768]{3,2,1,0:T(8,128)(2,1)} %bitcast.11), calls=%async_computation.1 | async-start | bytes 3145728 | tf_op jit(solution)/shard_map/all_to_all | solution.py:224
  444.2 150.6 %copy-start.7 = (s32[256]{0:T(256)S(1)}, s32[256]{0:T(256)}, u32[]{:S(2)}) copy-start(s32[256]{0:T(256)} %param.10) | copy-start | bytes 3076
  444.2 154.4 %copy-start.4 = (f32[1,2048]{1,0:T(1,128)S(1)}, f32[1,2048]{1,0:T(1,128)}, u32[]{:S(2)}) copy-start(f32[1,2048]{1,0:T(1,128)} %weight_ref.7) | copy-start | bytes 24580
  444.2 154.4 %copy-start.5 = (s32[4]{0:T(128)S(1)}, s32[4]{0:T(128)}, u32[]{:S(2)}) copy-start(s32[4]{0:T(128)} %live_ref.7) | copy-start | bytes 52
  589.6 56.5 %all-to-all-start = ((bf16[8,4,32,768]{3,2,1,0:T(8,128)(2,1)}), bf16[8,4,32,768]{3,2,1,0:T(8,128)(2,1)}, u32[]{:S(2)}, u32[]{:S(2)}) async-start(bf16[8,4,32,768]{3,2,1,0:T(8,128)(2,1)} %bitcast.7), calls=%async_computation | async-start | bytes 3145728 | tf_op jit(solution)/shard_map/all_to_all | solution.py:224
  598.6 2.8 copy-start.1
  614.9 2.8 copy-start.2
  646.1 2.8 copy-start.3
Sparse Core Ops, SparseCore 0:
  13.1 119.4 all-gather.14
  134.2 120.4 all-gather.12
  256.3 161.5 all-gather.10
  419.4 148.3 all-gather.8

commit v2 on v1

--- a/solution.py
+++ b/solution.py
@@ -16,7 +16,9 @@
 norm_eps = 1e-05
 
 
-def permute_kernel(order_ref, rows_ref, out_ref):
+def permute_kernel(order_ref, rows_ref, *refs):
+    out_ref = refs[-1]
+
     def move(slot, carry):
         out_ref[slot] = rows_ref[order_ref[slot]]
         return carry
@@ -24,7 +26,7 @@
     lax.fori_loop(0, out_ref.shape[0], move, 0)
 
 
-def permute_steps(order, rows):
+def permute_steps(order, rows, after):
     size = rows.size * rows.dtype.itemsize
     return pl.pallas_call(
         permute_kernel,
@@ -32,11 +34,12 @@
         in_specs=[
             pl.BlockSpec(memory_space=pltpu.SMEM),
             pl.BlockSpec(memory_space=pltpu.VMEM),
-        ],
+        ]
+        + [pl.BlockSpec(memory_space=pl.ANY)] * len(after),
         out_specs=pl.BlockSpec(memory_space=pltpu.VMEM),
         compiler_params=pltpu.CompilerParams(vmem_limit_bytes=2 * size + (4 << 20)),
         cost_estimate=pl.CostEstimate(flops=0, bytes_accessed=2 * size, transcendentals=0),
-    )(order, rows)
+    )(order, rows, *after)
 
 
 def attend_kernel(
@@ -163,6 +166,18 @@
     )(arrange, lengths, live, *operands)
 
 
+def sum_over(value, axis):
+    count = lax.axis_size(axis)
+    if count & (count - 1):
+        return lax.psum(value, axis)
+    reach = 1
+    while reach < count:
+        hops = [(i, i ^ reach) for i in range(count)]
+        value = value + lax.ppermute(value, axis, hops)
+        reach *= 2
+    return value
+
+
 def per_device(
     step_embeds, step_len, leaf_of_step, cache_len, caches, norm_gain, qkv_weight, score_weight
 ):
@@ -182,12 +197,7 @@
 
     own = embeds.reshape(steps_here * seq_max, piece_width)
     width = (group_size + 2) * HD
-    gathered = [
-        lax.all_gather(
-            qkv_weight[0, :, g * width : (g + 1) * width], "dp", axis=0, tiled=True
-        )
-        for g in range(groups)
-    ]
+    gathered = lax.all_gather(qkv_weight[0], "dp", axis=0, tiled=True)
     local_rows = jnp.zeros((steps_here * seq_max, row_width), own.dtype)
     for shift in range(tensor_count):
         source = lax.rem(tensor_index + tensor_count - shift, tensor_count)
@@ -215,20 +225,26 @@
     inverse_rms = lax.rsqrt(jnp.mean(as_float * as_float, axis=-1, keepdims=True) + norm_eps)
     normed = (as_float * inverse_rms * norm_gain[0]).astype(jnp.bfloat16)
 
+    normed = lax.optimization_barrier(normed)
     contexts, partial_value = None, 0.0
+    after = [(arrange, lengths), ()]
     for g in range(groups):
-        summed = jnp.dot(normed, gathered[g], preferred_element_type=jnp.float32)
+        weight = gathered[:, g * width : (g + 1) * width]
+        summed = jnp.dot(normed, weight, preferred_element_type=jnp.float32)
         outbound = summed.astype(jnp.bfloat16).reshape(steps_here, seq_max, width)
-        outbound = permute_steps(send_order, outbound)
+        outbound = permute_steps(send_order, outbound, after[g])
         outbound = outbound.reshape(part_count, per_peer, seq_max, width)
         arrived = lax.all_to_all(outbound, "dp", split_axis=0, concat_axis=0, tiled=True)
         arrived = arrived.reshape(steps_here, seq_max, width)
         contexts, shares = attend(
             g, groups, per_leaf, arrange, lengths, cache_len, arrived, caches, score_weight, contexts
         )
+        after.append((shares,))
         partial_value = partial_value + jnp.sum(shares, axis=-1)
     model_weight = jnp.where(lax.axis_index("mp") == 0, prior_weight, 1.0).astype(jnp.float32)
-    step_value = lax.psum(partial_value * model_weight, ("tensor", "mp"))
+    step_value = partial_value * model_weight
+    for axis in ("tensor", "mp"):
+        step_value = sum_over(step_value, axis)
     return (contexts, step_value)
 
 

time: 682 us -> 661 us (0.969)
  waiting for transfers between devices: 441 us -> 421 us
  blocking collectives: 10.4 us -> 0 us
  other arithmetic: 10.8 us -> 20 us
    all_gather x4 -> x1, waiting for transfers between devices: 246 us -> 221 us  [per_device(): gathered = lax.all_gather(qkv_weight[0], 'dp', axis=0, tiled=True)]
    psum x1 -> x0, blocking collectives: 10.4 us -> none  [per_device(): step_value = lax.psum(partial_value * model_weight, ('tensor', 'mp'))]
    all_to_all x4, waiting for transfers between devices: 30.1 us -> 40.1 us  [per_device(): lax.all_to_all(outbound, 'dp', split_axis=0, concat_axis=0, tiled=True)]
    ppermute x1, waiting for transfers between devices: 164 us -> 155 us  [per_device(): piece = lax.ppermute(own, 'tensor', hops)]
    convert_element_type x0 -> x1, other arithmetic: none -> 8.17 us  [per_device(): normed = (as_float * inverse_rms * norm_gain[0]).astype(jnp.bfloat16)]
  transfers between devices with their start and end apart: 9 -> 8, of which waited for: 5 -> 7; matrix products, arithmetic and copies ran while one was open for 17% -> 16% of each run, Pallas kernels for 7% -> 7%
where the time goes in v2:
time: 661 us
  waiting for transfers between devices  421 us (64%)
  matrix products  75 us (11%)
  Pallas kernels  63.5 us (10%)
  local copies, waits for them, and re-layouts  43.3 us (7%)
  starting transfers between devices  23.7 us (4%)
  other arithmetic  20 us (3%)
  between operations  14.3 us (2%)
    all_gather x1, waiting for transfers between devices, per_device(): gathered = lax.all_gather(qkv_weight[0], 'dp', axis=0, tiled=True)  221 us
    ppermute x1, waiting for transfers between devices, per_device(): piece = lax.ppermute(own, 'tensor', hops)  155 us
    dot_general x4, matrix products, per_device(): summed = jnp.dot(normed, weight, preferred_element_type=jnp.float32)  75 us
    pallas_call x4, Pallas kernels, attend(): pl.pallas_call(functools.partial(attend_kernel, per_leaf, group_size), gr...  56.7 us
    all_to_all x4, waiting for transfers between devices, per_device(): lax.all_to_all(outbound, 'dp', split_axis=0, concat_axis=0, tiled=True)  40.1 us
    all_to_all x4, starting transfers between devices, per_device(): lax.all_to_all(outbound, 'dp', split_axis=0, concat_axis=0, tiled=True)  17.6 us
    dynamic_update_slice x2, local copies, waits for them, and re-layouts, per_device(): lax.dynamic_update_slice_in_dim(local_rows, piece, source * piece_width, 1)  17.6 us
  transfers between devices with their start and end apart: 8, of which 7 were waited for; matrix products, arithmetic and copies ran while one was open for 16% of the time, Pallas kernels for 7%

profile of v2, /device:TPU:0, one launch (start us, length us, event | category | flops | bytes accessed | tf_op | source)
XLA Modules:
  0.0 660.6 jit_solution(17806938992047427870)
XLA Ops:
  7.9 3.0 collective-permute-start
  17.5 9.4 %broadcast_in_dim.5 = bf16[1024,8192]{1,0:T(8,128)(2,1)} broadcast(bf16[]{:T(256)} %constant.59.clone.1), dimensions={} | broadcast | bytes 16777218 | tf_op jit(solution)/shard_map/broadcast_in_dim | solution.py:201
  26.9 9.8 %constant_dynamic-update-slice_fusion.1 = bf16[1024,8192]{1,0:T(8,128)(2,1)} fusion(bf16[1024,8192]{1,0:T(8,128)(2,1)} %broadcast_in_dim.5, bf16[1024,4096]{1,0:T(8,128)(2,1)} %bitcast.35, s32[]{:T(128)S(6)} %select_n.51), kind=kLoop, calls=%fused_computation.36 | loop fusion | bytes 16777220 | tf_op jit(solution)/shard_map/dynamic_update_slice | solution.py:208
  36.8 154.9 %collective-permute-done = bf16[1024,4096]{1,0:T(8,128)(2,1)} collective-permute-done((bf16[1024,4096]{1,0:T(8,128)(2,1)}, bf16[1024,4096]{1,0:T(8,128)(2,1)}, u32[]{:S(2)}, u32[]{:S(2)}) %collective-permute-start) | collective-permute-done | bytes 8388640 | tf_op jit(solution)/shard_map/ppermute | solution.py:207
  191.7 7.7 %constant_dynamic-update-slice_fusion = bf16[1024,8192]{1,0:T(8,128)(2,1)} fusion(bf16[1024,8192]{1,0:T(8,128)(2,1)} %constant_dynamic-update-slice_fusion.1, bf16[1024,4096]{1,0:T(8,128)(2,1)} %collective-permute-done, s32[]{:T(128)S(6)} %select_n.52), kind=kLoop, calls=%fused_computation.35 | loop fusion | bytes 16777220 | tf_op jit(solution)/shard_map/dynamic_update_slice | solution.py:208
  199.5 7.8 %fusion = f32[1024]{0:T(1024)S(1)} fusion(bf16[1024,8192]{1,0:T(8,128)(2,1)} %constant_dynamic-update-slice_fusion), kind=kLoop, calls=%fused_computation.5 | loop fusion | flops 25164800 | bytes 16781312 | tf_op jit(solution)/shard_map/reduce_sum | solution.py:225
  207.3 3.4 copy-done.8
  210.6 8.2 %fusion.2 = bf16[1024,8192]{1,0:T(8,128)(2,1)} fusion(bf16[1024,8192]{1,0:T(8,128)(2,1)S(1)} %copy-done.8, f32[8192]{0:T(1024)S(1)} %bitcast.36, f32[1024]{0:T(1024)S(1)} %add_rsqrt_fusion), kind=kLoop, calls=%fused_computation.7 | loop fusion | flops 33554432 | bytes 33591296 | tf_op jit(solution)/shard_map/convert_element_type | solution.py:226
  218.8 221.0 %all-gather.3.cloned.1.call-done = bf16[1,8192,3072]{2,1,0:T(8,128)(2,1)} async-done(((bf16[1,1024,3072]{2,1,0:T(8,128)(2,1)}), bf16[1,8192,3072]{2,1,0:T(8,128)(2,1)}) %all-gather.3.cloned.1.call-update) | async-done | bytes 50331664 | tf_op jit(solution)/shard_map/all_gather | solution.py:200
  439.8 18.7 %fusion.17 = bf16[1024,768]{1,0:T(8,128)(2,1)S(1)} fusion(bf16[1024,8192]{1,0:T(8,128)(2,1)} %fusion.2, bf16[8192,3072]{1,0:T(8,128)(2,1)} %bitcast.37), kind=kOutput, calls=%fused_computation.18 | convolution fusion | flops 12885688320 | bytes 30932992 | tf_op jit(solution)/shard_map/dot_general | solution.py:233
  458.5 2.0 shard_map.96
  460.4 4.5 all-to-all-start.1
  464.9 18.8 %fusion.14 = bf16[1024,768]{1,0:T(8,128)(2,1)S(1)} fusion(bf16[1024,8192]{1,0:T(8,128)(2,1)} %fusion.2, bf16[8192,3072]{1,0:T(8,128)(2,1)} %bitcast.38), kind=kOutput, calls=%fused_computation.17 | convolution fusion | flops 12885688320 | bytes 30932992 | tf_op jit(solution)/shard_map/dot_general | solution.py:233
  485.7 16.9 %all-to-all-done.1 = bf16[8,4,32,768]{3,2,1,0:T(8,128)(2,1)} async-done(((bf16[8,4,32,768]{3,2,1,0:T(8,128)(2,1)}), bf16[8,4,32,768]{3,2,1,0:T(8,128)(2,1)}, u32[]{:S(2)}, u32[]{:S(2)}) %all-to-all-start.1) | async-done | bytes 1572896 | tf_op jit(solution)/shard_map/all_to_all | solution.py:237
  502.6 4.5 all-to-all-start
  507.1 18.8 %fusion.20 = bf16[1024,768]{1,0:T(8,128)(2,1)S(1)} fusion(bf16[1024,8192]{1,0:T(8,128)(2,1)} %fusion.2, bf16[8192,3072]{1,0:T(8,128)(2,1)} %bitcast.39), kind=kOutput, calls=%fused_computation.19 | convolution fusion | flops 12885688320 | bytes 30932992 | tf_op jit(solution)/shard_map/dot_general | solution.py:233
  526.0 14.9 %shard_map.97 = (bf16[1,4,8,32,2048]{4,3,2,1,0:T(8,128)(2,1)}, f32[4,8,128]{2,1,0:T(8,128)S(1)}) custom-call(s32[32]{0:T(128)S(1)} %get-tuple-element.13.refs_0_.arrange_ref, s32[32]{0:T(128)S(1)} %gather_fusion.2, s32[4]{0:T(128)S(1)} %copy-done.7, bf16[32,32,768]{2,1,0:T(8,128)(2,1)} %bitcast.12.rows_ref, bf16[1,4,768,1024]{3,2,1,0:T(8,128)(2,1)S(1)} %bitcast.26, ...), custom_call_target="tpu_custom_call" | custom-call | flops 1879048192 | bytes 8388608 | tf_op jit(solution)/shard_map/pallas_call | solution.py:137
  540.9 2.0 shard_map.100
  542.9 1.8 all-to-all-done
  544.7 3.8 all-to-all-start.3
  548.6 18.7 %fusion.11 = bf16[1024,768]{1,0:T(8,128)(2,1)S(1)} fusion(bf16[1024,8192]{1,0:T(8,128)(2,1)} %fusion.2, bf16[8192,3072]{1,0:T(8,128)(2,1)} %bitcast.40), kind=kOutput, calls=%fused_computation.16 | convolution fusion | flops 12885688320 | bytes 30932992 | tf_op jit(solution)/shard_map/dot_general | solution.py:233
  567.3 2.8 copy-done.2
  570.1 14.9 %shard_map.98 = (bf16[1,4,8,32,2048]{4,3,2,1,0:T(8,128)(2,1)}, f32[4,8,128]{2,1,0:T(8,128)S(1)}) custom-call(s32[32]{0:T(128)S(1)} %get-tuple-element.13.refs_0_.arrange_ref, s32[32]{0:T(128)S(1)} %gather_fusion.2, s32[4]{0:T(128)S(1)} %copy-done.7, bf16[32,32,768]{2,1,0:T(8,128)(2,1)} %bitcast.9.rows_ref, ...), custom_call_target="tpu_custom_call", output_to_operand_aliasing={{0}: (6, {})} | custom-call | flops 1879048192 | bytes 8388608 | tf_op jit(solution)/shard_map/pallas_call | solution.py:137
  584.9 2.0 shard_map.99
  586.9 4.8 all-to-all-start.2
  591.8 2.8 copy-done.3
  594.6 13.5 %shard_map.101 = (bf16[1,4,8,32,2048]{4,3,2,1,0:T(8,128)(2,1)}, f32[4,8,128]{2,1,0:T(8,128)S(1)}) custom-call(s32[32]{0:T(128)S(1)} %get-tuple-element.13.refs_0_.arrange_ref, s32[32]{0:T(128)S(1)} %gather_fusion.2, s32[4]{0:T(128)S(1)} %copy-done.7, bf16[32,32,768]{2,1,0:T(8,128)(2,1)S(1)} %bitcast.28, ...), custom_call_target="tpu_custom_call", output_to_operand_aliasing={{0}: (6, {})} | custom-call | flops 1879048192 | bytes 8388608 | tf_op jit(solution)/shard_map/pallas_call | solution.py:137
  608.1 21.4 %all-to-all-done.2 = bf16[8,4,32,768]{3,2,1,0:T(8,128)(2,1)S(1)} async-done(((bf16[8,4,32,768]{3,2,1,0:T(8,128)(2,1)}), bf16[8,4,32,768]{3,2,1,0:T(8,128)(2,1)S(1)}, u32[]{:S(2)}, u32[]{:S(2)}) %all-to-all-start.2) | async-done | bytes 1572896 | tf_op jit(solution)/shard_map/all_to_all | solution.py:237
  629.5 2.8 copy-done.4
  632.3 13.5 %shard_map.102 = (bf16[1,4,8,32,2048]{4,3,2,1,0:T(8,128)(2,1)}, f32[4,8,128]{2,1,0:T(8,128)S(1)}) custom-call(s32[32]{0:T(128)S(1)} %get-tuple-element.13.refs_0_.arrange_ref, s32[32]{0:T(128)S(1)} %gather_fusion.2, s32[4]{0:T(128)S(1)} %copy-done.7, bf16[32,32,768]{2,1,0:T(8,128)(2,1)S(1)} %bitcast.29, ...), custom_call_target="tpu_custom_call", output_to_operand_aliasing={{0}: (6, {})} | custom-call | flops 1879048192 | bytes 8388608 | tf_op jit(solution)/shard_map/pallas_call | solution.py:137
  647.5 2.1 collective-permute-done.1
  651.1 2.1 collective-permute-done.2
  (59 shorter events, 13.2 us)
Async XLA Ops:
  7.2 9.5 %copy-start = (s32[256]{0:T(256)S(1)}, s32[256]{0:T(256)}, u32[]{:S(2)}) copy-start(s32[256]{0:T(256)} %param.9) | copy-start | bytes 3076
  7.2 432.6 %all-gather.3.cloned.1.call-start = ((), (), s32[]{:S(2)}) async-start(), calls=%async_computation.4 | async-start | bytes 56623104 | tf_op jit(solution)/shard_map/all_gather | solution.py:200
  7.9 183.8 %collective-permute-start = (bf16[1024,4096]{1,0:T(8,128)(2,1)}, bf16[1024,4096]{1,0:T(8,128)(2,1)}, u32[]{:S(2)}, u32[]{:S(2)}) collective-permute-start(bf16[1024,4096]{1,0:T(8,128)(2,1)} %bitcast.34), channel_id=1, source_target_pairs={{0,2},{2,0},{1,3},{3,1},{4,6},{6,4},{5,7},{7,5},{8,10},{10,8},{9,1... | collective-permute-start | bytes 25165832 | tf_op jit(solution)/shard_map/ppermute | solution.py:207
  36.8 170.5 %copy-start.9 = (f32[1,8192]{1,0:T(1,128)S(1)}, f32[1,8192]{1,0:T(1,128)}, u32[]{:S(2)}) copy-start(f32[1,8192]{1,0:T(1,128)} %param.13) | copy-start | bytes 98308
  199.5 11.2 %copy-start.8 = (bf16[1024,8192]{1,0:T(8,128)(2,1)S(1)}, bf16[1024,8192]{1,0:T(8,128)(2,1)}, u32[]{:S(2)}) copy-start(bf16[1024,8192]{1,0:T(8,128)(2,1)} %constant_dynamic-update-slice_fusion) | copy-start | bytes 50331652
  460.4 42.1 %all-to-all-start.1 = ((bf16[8,4,32,768]{3,2,1,0:T(8,128)(2,1)}), bf16[8,4,32,768]{3,2,1,0:T(8,128)(2,1)}, u32[]{:S(2)}, u32[]{:S(2)}) async-start(bf16[8,4,32,768]{3,2,1,0:T(8,128)(2,1)} %bitcast.11), calls=%async_computation.1 | async-start | bytes 3145728 | tf_op jit(solution)/shard_map/all_to_all | solution.py:237
  483.7 42.3 %slice-start = ((s8[6291456]{0:T(1024)(128)(4,1)}), s8[2097152]{0:T(1024)(128)(4,1)S(1)}, s32[]{:S(2)}) async-start(s8[6291456]{0:T(1024)(128)(4,1)} %bitcast.25), calls=%async_computation.5 | async-start | bytes 4194304
  484.5 1.1 copy-start.5
  502.6 42.1 %all-to-all-start = ((bf16[8,4,32,768]{3,2,1,0:T(8,128)(2,1)}), bf16[8,4,32,768]{3,2,1,0:T(8,128)(2,1)}, u32[]{:S(2)}, u32[]{:S(2)}) async-start(bf16[8,4,32,768]{3,2,1,0:T(8,128)(2,1)} %bitcast.27), calls=%async_computation | async-start | bytes 3145728 | tf_op jit(solution)/shard_map/all_to_all | solution.py:237
  507.1 18.9 %slice-start.1 = ((s8[6291456]{0:T(1024)(128)(4,1)}), s8[4194304]{0:T(1024)(128)(4,1)S(1)}, s32[]{:S(2)}) async-start(s8[6291456]{0:T(1024)(128)(4,1)} %bitcast.25), calls=%async_computation.6 | async-start | bytes 8388608
  507.1 18.9 %copy-start.6 = (f32[1,2048]{1,0:T(1,128)S(1)}, f32[1,2048]{1,0:T(1,128)}, u32[]{:S(2)}) copy-start(f32[1,2048]{1,0:T(1,128)} %weight_ref.7) | copy-start | bytes 24580
  507.1 18.9 %copy-start.7 = (s32[4]{0:T(128)S(1)}, s32[4]{0:T(128)}, u32[]{:S(2)}) copy-start(s32[4]{0:T(128)} %live_ref.7) | copy-start | bytes 52
  544.7 42.2 %all-to-all-start.3 = ((bf16[8,4,32,768]{3,2,1,0:T(8,128)(2,1)}), bf16[8,4,32,768]{3,2,1,0:T(8,128)(2,1)S(1)}, u32[]{:S(2)}, u32[]{:S(2)}) async-start(bf16[8,4,32,768]{3,2,1,0:T(8,128)(2,1)} %bitcast.16), calls=%async_computation.3 | async-start | bytes 3145728 | tf_op jit(solution)/shard_map/all_to_all | solution.py:237
  567.3 2.8 copy-start.2
  570.1 83.7 %copy-start.1 = (s32[256]{0:T(256)S(1)}, s32[256]{0:T(256)}, u32[]{:S(2)}) copy-start(s32[256]{0:T(256)} %param.9) | copy-start | bytes 3076
  586.9 42.6 %all-to-all-start.2 = ((bf16[8,4,32,768]{3,2,1,0:T(8,128)(2,1)}), bf16[8,4,32,768]{3,2,1,0:T(8,128)(2,1)S(1)}, u32[]{:S(2)}, u32[]{:S(2)}) async-start(bf16[8,4,32,768]{3,2,1,0:T(8,128)(2,1)} %bitcast.13), calls=%async_computation.2 | async-start | bytes 3145728 | tf_op jit(solution)/shard_map/all_to_all | solution.py:237
  591.8 2.8 copy-start.3
  629.5 2.8 copy-start.4
  646.0 3.6 collective-permute-start.1
  649.6 3.6 collective-permute-start.2
Sparse Core Ops, SparseCore 0:
  9.7 430.0 all-gather.2

commit v3 on v2

--- a/solution.py
+++ b/solution.py
@@ -197,7 +197,14 @@
 
     own = embeds.reshape(steps_here * seq_max, piece_width)
     width = (group_size + 2) * HD
-    gathered = lax.all_gather(qkv_weight[0], "dp", axis=0, tiled=True)
+    split = max(groups - 1, 1)
+    bounds = [(0, split)] + ([(split, groups)] if split < groups else [])
+    gathered = [
+        lax.all_gather(
+            qkv_weight[0, :, start * width : end * width], "dp", axis=0, tiled=True
+        )
+        for start, end in bounds
+    ]
     local_rows = jnp.zeros((steps_here * seq_max, row_width), own.dtype)
     for shift in range(tensor_count):
         source = lax.rem(tensor_index + tensor_count - shift, tensor_count)
@@ -229,10 +236,12 @@
     contexts, partial_value = None, 0.0
     after = [(arrange, lengths), ()]
     for g in range(groups):
-        weight = gathered[:, g * width : (g + 1) * width]
+        part = 0 if g < split else 1
+        place = g - bounds[part][0]
+        weight = gathered[part][:, place * width : (place + 1) * width]
         summed = jnp.dot(normed, weight, preferred_element_type=jnp.float32)
         outbound = summed.astype(jnp.bfloat16).reshape(steps_here, seq_max, width)
-        outbound = permute_steps(send_order, outbound, after[g])
+        outbound = permute_steps(send_order, outbound, after[g] if g < split else ())
         outbound = outbound.reshape(part_count, per_peer, seq_max, width)
         arrived = lax.all_to_all(outbound, "dp", split_axis=0, concat_axis=0, tiled=True)
         arrived = arrived.reshape(steps_here, seq_max, width)

time: 661 us -> 632 us (0.956)
  waiting for transfers between devices: 421 us -> 387 us
    all_gather x1 -> x2, waiting for transfers between devices: 221 us -> 120 us  [per_device(): lax.all_gather(qkv_weight[0, :, start * width:end * width], 'dp', axis=0,...]
    all_to_all x4, waiting for transfers between devices: 40.1 us -> 108 us  [per_device(): lax.all_to_all(outbound, 'dp', split_axis=0, concat_axis=0, tiled=True)]
    slice x0 -> x2, local copies, waits for them, and re-layouts: none -> 7.5 us  [per_device(): qkv_weight[0, :, start * width:end * width]]
  transfers between devices with their start and end apart: 8 -> 9, of which waited for: 7 -> 9; matrix products, arithmetic and copies ran while one was open for 16% -> 20% of each run, Pallas kernels for 7% -> 8%
where the time goes in v3:
time: 632 us; the launch traced here: 631 us
  waiting for transfers between devices  387 us (61%)
  matrix products  75.1 us (12%)
  Pallas kernels  63.5 us (10%)
  local copies, waits for them, and re-layouts  49.7 us (8%)
  starting transfers between devices  22.8 us (4%)
  other arithmetic  19.2 us (3%)
  between operations  14.3 us (2%)
    ppermute x1, waiting for transfers between devices, per_device(): piece = lax.ppermute(own, 'tensor', hops)  154 us
    all_gather x2, waiting for transfers between devices, per_device(): lax.all_gather(qkv_weight[0, :, start * width:end * width], 'dp', axis=0,...  120 us
    all_to_all x4, waiting for transfers between devices, per_device(): lax.all_to_all(outbound, 'dp', split_axis=0, concat_axis=0, tiled=True)  108 us
    dot_general x4, matrix products, per_device(): summed = jnp.dot(normed, weight, preferred_element_type=jnp.float32)  75.1 us
    pallas_call x4, Pallas kernels, attend(): pl.pallas_call(functools.partial(attend_kernel, per_leaf, group_size), gr...  56.8 us
    dynamic_update_slice x2, local copies, waits for them, and re-layouts, per_device(): lax.dynamic_update_slice_in_dim(local_rows, piece, source * piece_width, 1)  18 us
    all_to_all x4, starting transfers between devices, per_device(): lax.all_to_all(outbound, 'dp', split_axis=0, concat_axis=0, tiled=True)  16.7 us
    unnamed x26, local copies, waits for them, and re-layouts  13 us
  transfers between devices with their start and end apart: 9, of which 9 were waited for; matrix products, arithmetic and copies ran while one was open for 20% of the time, Pallas kernels for 8%

profile of v3, /device:TPU:0, one launch (start us, length us, event | category | flops | bytes accessed | tf_op | source)
XLA Modules:
  0.0 631.4 jit_solution(11090920749618962064)
XLA Ops:
  7.2 4.8 slice.16
  12.1 3.0 collective-permute-start
  15.2 2.7 slice.15
  23.1 8.4 %broadcast_in_dim.5 = bf16[1024,8192]{1,0:T(8,128)(2,1)} broadcast(bf16[]{:T(256)} %constant.59.clone.1), dimensions={} | broadcast | bytes 16777218 | tf_op jit(solution)/shard_map/broadcast_in_dim | solution.py:208
  31.5 10.2 %constant_dynamic-update-slice_fusion.1 = bf16[1024,8192]{1,0:T(8,128)(2,1)} fusion(bf16[1024,8192]{1,0:T(8,128)(2,1)} %broadcast_in_dim.5, bf16[1024,4096]{1,0:T(8,128)(2,1)} %bitcast.40, s32[]{:T(128)S(6)} %select_n.51), kind=kLoop, calls=%fused_computation.36 | loop fusion | bytes 16777220 | tf_op jit(solution)/shard_map/dynamic_update_slice | solution.py:215
  41.7 154.2 %collective-permute-done = bf16[1024,4096]{1,0:T(8,128)(2,1)} collective-permute-done((bf16[1024,4096]{1,0:T(8,128)(2,1)}, bf16[1024,4096]{1,0:T(8,128)(2,1)}, u32[]{:S(2)}, u32[]{:S(2)}) %collective-permute-start) | collective-permute-done | bytes 8388640 | tf_op jit(solution)/shard_map/ppermute | solution.py:214
  195.9 7.8 %constant_dynamic-update-slice_fusion = bf16[1024,8192]{1,0:T(8,128)(2,1)} fusion(bf16[1024,8192]{1,0:T(8,128)(2,1)} %constant_dynamic-update-slice_fusion.1, bf16[1024,4096]{1,0:T(8,128)(2,1)} %collective-permute-done, s32[]{:T(128)S(6)} %select_n.52), kind=kLoop, calls=%fused_computation.35 | loop fusion | bytes 16777220 | tf_op jit(solution)/shard_map/dynamic_update_slice | solution.py:215
  203.8 7.4 %fusion = f32[1024]{0:T(1024)S(1)} fusion(bf16[1024,8192]{1,0:T(8,128)(2,1)} %constant_dynamic-update-slice_fusion), kind=kLoop, calls=%fused_computation.5 | loop fusion | flops 25164800 | bytes 16781312 | tf_op jit(solution)/shard_map/reduce_sum | solution.py:232
  211.3 3.5 copy-done.9
  214.7 8.3 %fusion.2 = bf16[1024,8192]{1,0:T(8,128)(2,1)} fusion(bf16[1024,8192]{1,0:T(8,128)(2,1)S(1)} %copy-done.9, f32[8192]{0:T(1024)S(1)} %bitcast.41, f32[1024]{0:T(1024)S(1)} %add_rsqrt_fusion), kind=kLoop, calls=%fused_computation.7 | loop fusion | flops 33554432 | bytes 33591296 | tf_op jit(solution)/shard_map/convert_element_type | solution.py:233
  223.0 117.2 %all-gather.7.cloned.1.call-done = bf16[1,8192,2304]{2,1,0:T(8,128)(2,1)} async-done(((bf16[1,1024,2304]{2,1,0:T(8,128)(2,1)}), bf16[1,8192,2304]{2,1,0:T(8,128)(2,1)}) %all-gather.7.cloned.1.call-update) | async-done | bytes 37748752 | tf_op jit(solution)/shard_map/all_gather | solution.py:203
  340.2 18.7 %fusion.17 = bf16[1024,768]{1,0:T(8,128)(2,1)S(1)} fusion(bf16[1024,8192]{1,0:T(8,128)(2,1)} %fusion.2, bf16[8192,2304]{1,0:T(8,128)(2,1)} %bitcast.42), kind=kOutput, calls=%fused_computation.18 | convolution fusion | flops 12885688320 | bytes 30932992 | tf_op jit(solution)/shard_map/dot_general | solution.py:242
  360.9 4.5 all-to-all-start.1
  365.4 18.8 %fusion.20 = bf16[1024,768]{1,0:T(8,128)(2,1)S(1)} fusion(bf16[1024,8192]{1,0:T(8,128)(2,1)} %fusion.2, bf16[8192,2304]{1,0:T(8,128)(2,1)} %bitcast.43), kind=kOutput, calls=%fused_computation.19 | convolution fusion | flops 12885688320 | bytes 30932992 | tf_op jit(solution)/shard_map/dot_general | solution.py:242
  386.2 59.4 %all-to-all-done.1 = bf16[8,4,32,768]{3,2,1,0:T(8,128)(2,1)} async-done(((bf16[8,4,32,768]{3,2,1,0:T(8,128)(2,1)}), bf16[8,4,32,768]{3,2,1,0:T(8,128)(2,1)}, u32[]{:S(2)}, u32[]{:S(2)}) %all-to-all-start.1) | async-done | bytes 1572896 | tf_op jit(solution)/shard_map/all_to_all | solution.py:246
  445.6 4.5 all-to-all-start.3
  450.2 18.8 %fusion.14 = bf16[1024,768]{1,0:T(8,128)(2,1)S(1)} fusion(bf16[1024,8192]{1,0:T(8,128)(2,1)} %fusion.2, bf16[8192,2304]{1,0:T(8,128)(2,1)} %bitcast.44), kind=kOutput, calls=%fused_computation.17 | convolution fusion | flops 12885688320 | bytes 30932992 | tf_op jit(solution)/shard_map/dot_general | solution.py:242
  469.1 14.9 %shard_map.97 = (bf16[1,4,8,32,2048]{4,3,2,1,0:T(8,128)(2,1)}, f32[4,8,128]{2,1,0:T(8,128)S(1)}) custom-call(s32[32]{0:T(128)S(1)} %get-tuple-element.13.refs_0_.arrange_ref, s32[32]{0:T(128)S(1)} %gather_fusion.2, s32[4]{0:T(128)S(1)} %copy-done.7, bf16[32,32,768]{2,1,0:T(8,128)(2,1)} %bitcast.13.rows_ref, bf16[1,4,768,1024]{3,2,1,0:T(8,128)(2,1)S(1)} %bitcast.31, ...), custom_call_target="tpu_custom_call" | custom-call | flops 1879048192 | bytes 8388608 | tf_op jit(solution)/shard_map/pallas_call | solution.py:137
  485.9 31.6 %all-to-all-done.3 = bf16[8,4,32,768]{3,2,1,0:T(8,128)(2,1)} async-done(((bf16[8,4,32,768]{3,2,1,0:T(8,128)(2,1)}), bf16[8,4,32,768]{3,2,1,0:T(8,128)(2,1)}, u32[]{:S(2)}, u32[]{:S(2)}) %all-to-all-start.3) | async-done | bytes 1572896 | tf_op jit(solution)/shard_map/all_to_all | solution.py:246
  517.6 3.8 all-to-all-start.2
  521.4 3.2 all-gather.5.cloned.1.call-done
  524.6 18.7 %fusion.11 = bf16[1024,768]{1,0:T(8,128)(2,1)S(1)} fusion(bf16[1024,8192]{1,0:T(8,128)(2,1)} %fusion.2, bf16[1,8192,768]{2,1,0:T(8,128)(2,1)} %all-gather.5.cloned.1.call-done), kind=kOutput, calls=%fused_computation.16 | convolution fusion | flops 12885688320 | bytes 30932992 | tf_op jit(solution)/shard_map/dot_general | solution.py:242
  545.3 13.6 %all-to-all-done.2 = bf16[8,4,32,768]{3,2,1,0:T(8,128)(2,1)S(1)} async-done(((bf16[8,4,32,768]{3,2,1,0:T(8,128)(2,1)}), bf16[8,4,32,768]{3,2,1,0:T(8,128)(2,1)S(1)}, u32[]{:S(2)}, u32[]{:S(2)}) %all-to-all-start.2) | async-done | bytes 1572896 | tf_op jit(solution)/shard_map/all_to_all | solution.py:246
  558.9 3.9 all-to-all-start
  562.9 2.8 copy-done.2
  565.7 14.9 %shard_map.100 = (bf16[1,4,8,32,2048]{4,3,2,1,0:T(8,128)(2,1)}, f32[4,8,128]{2,1,0:T(8,128)S(1)}) custom-call(s32[32]{0:T(128)S(1)} %get-tuple-element.13.refs_0_.arrange_ref, s32[32]{0:T(128)S(1)} %gather_fusion.2, s32[4]{0:T(128)S(1)} %copy-done.7, bf16[32,32,768]{2,1,0:T(8,128)(2,1)} %bitcast.18.rows_ref, ...), custom_call_target="tpu_custom_call", output_to_operand_aliasing={{0}: (6, {})} | custom-call | flops 1879048192 | bytes 8388608 | tf_op jit(solution)/shard_map/pallas_call | solution.py:137
  580.6 2.8 copy-done.3
  583.4 13.5 %shard_map.101 = (bf16[1,4,8,32,2048]{4,3,2,1,0:T(8,128)(2,1)}, f32[4,8,128]{2,1,0:T(8,128)S(1)}) custom-call(s32[32]{0:T(128)S(1)} %get-tuple-element.13.refs_0_.arrange_ref, s32[32]{0:T(128)S(1)} %gather_fusion.2, s32[4]{0:T(128)S(1)} %copy-done.7, bf16[32,32,768]{2,1,0:T(8,128)(2,1)S(1)} %bitcast.33, ...), custom_call_target="tpu_custom_call", output_to_operand_aliasing={{0}: (6, {})} | custom-call | flops 1879048192 | bytes 8388608 | tf_op jit(solution)/shard_map/pallas_call | solution.py:137
  596.9 3.3 all-to-all-done
  600.2 2.8 copy-done.4
  603.0 13.5 %shard_map.102 = (bf16[1,4,8,32,2048]{4,3,2,1,0:T(8,128)(2,1)}, f32[4,8,128]{2,1,0:T(8,128)S(1)}) custom-call(s32[32]{0:T(128)S(1)} %get-tuple-element.13.refs_0_.arrange_ref, s32[32]{0:T(128)S(1)} %gather_fusion.2, s32[4]{0:T(128)S(1)} %copy-done.7, bf16[32,32,768]{2,1,0:T(8,128)(2,1)S(1)} %bitcast.34, ...), custom_call_target="tpu_custom_call", output_to_operand_aliasing={{0}: (6, {})} | custom-call | flops 1879048192 | bytes 8388608 | tf_op jit(solution)/shard_map/pallas_call | solution.py:137
  621.8 2.1 collective-permute-done.2
  (66 shorter events, 19.3 us)
Async XLA Ops:
  7.2 15.1 %copy-start = (s32[256]{0:T(256)S(1)}, s32[256]{0:T(256)}, u32[]{:S(2)}) copy-start(s32[256]{0:T(256)} %param.9) | copy-start | bytes 3076
  7.2 10.7 %copy-start.8 = (s32[256]{0:T(256)S(1)}, s32[256]{0:T(256)}, u32[]{:S(2)}) copy-start(s32[256]{0:T(256)} %param.10) | copy-start | bytes 3076
  7.2 333.0 %all-gather.7.cloned.1.call-start = ((), (), s32[]{:S(2)}) async-start(), calls=%async_computation.5 | async-start | bytes 42467328 | tf_op jit(solution)/shard_map/all_gather | solution.py:203
  12.1 512.6 %all-gather.5.cloned.1.call-start = ((), (), s32[]{:S(2)}) async-start(), calls=%async_computation.4 | async-start | bytes 14155776 | tf_op jit(solution)/shard_map/all_gather | solution.py:203
  12.1 183.8 %collective-permute-start = (bf16[1024,4096]{1,0:T(8,128)(2,1)}, bf16[1024,4096]{1,0:T(8,128)(2,1)}, u32[]{:S(2)}, u32[]{:S(2)}) collective-permute-start(bf16[1024,4096]{1,0:T(8,128)(2,1)} %bitcast.39), channel_id=1, source_target_pairs={{0,2},{2,0},{1,3},{3,1},{4,6},{6,4},{5,7},{7,5},{8,10},{10,8},{9,1... | collective-permute-start | bytes 25165832 | tf_op jit(solution)/shard_map/ppermute | solution.py:214
  195.9 15.3 %copy-start.10 = (f32[1,8192]{1,0:T(1,128)S(1)}, f32[1,8192]{1,0:T(1,128)}, u32[]{:S(2)}) copy-start(f32[1,8192]{1,0:T(1,128)} %param.13) | copy-start | bytes 98308
  203.8 10.9 %copy-start.9 = (bf16[1024,8192]{1,0:T(8,128)(2,1)S(1)}, bf16[1024,8192]{1,0:T(8,128)(2,1)}, u32[]{:S(2)}) copy-start(bf16[1024,8192]{1,0:T(8,128)(2,1)} %constant_dynamic-update-slice_fusion) | copy-start | bytes 50331652
  360.9 84.8 %all-to-all-start.1 = ((bf16[8,4,32,768]{3,2,1,0:T(8,128)(2,1)}), bf16[8,4,32,768]{3,2,1,0:T(8,128)(2,1)}, u32[]{:S(2)}, u32[]{:S(2)}) async-start(bf16[8,4,32,768]{3,2,1,0:T(8,128)(2,1)} %bitcast.12), calls=%async_computation.1 | async-start | bytes 3145728 | tf_op jit(solution)/shard_map/all_to_all | solution.py:246
  384.2 84.8 %slice-start = ((s8[6291456]{0:T(1024)(128)(4,1)}), s8[2097152]{0:T(1024)(128)(4,1)S(1)}, s32[]{:S(2)}) async-start(s8[6291456]{0:T(1024)(128)(4,1)} %bitcast.30), calls=%async_computation.6 | async-start | bytes 4194304
  385.0 1.2 copy-start.5
  445.6 71.9 %all-to-all-start.3 = ((bf16[8,4,32,768]{3,2,1,0:T(8,128)(2,1)}), bf16[8,4,32,768]{3,2,1,0:T(8,128)(2,1)}, u32[]{:S(2)}, u32[]{:S(2)}) async-start(bf16[8,4,32,768]{3,2,1,0:T(8,128)(2,1)} %bitcast.32), calls=%async_computation.3 | async-start | bytes 3145728 | tf_op jit(solution)/shard_map/all_to_all | solution.py:246
  450.1 18.9 %slice-start.1 = ((s8[6291456]{0:T(1024)(128)(4,1)}), s8[4194304]{0:T(1024)(128)(4,1)S(1)}, s32[]{:S(2)}) async-start(s8[6291456]{0:T(1024)(128)(4,1)} %bitcast.30), calls=%async_computation.7 | async-start | bytes 8388608
  450.1 18.9 %copy-start.6 = (f32[1,2048]{1,0:T(1,128)S(1)}, f32[1,2048]{1,0:T(1,128)}, u32[]{:S(2)}) copy-start(f32[1,2048]{1,0:T(1,128)} %weight_ref.7) | copy-start | bytes 24580
  450.2 18.9 %copy-start.7 = (s32[4]{0:T(128)S(1)}, s32[4]{0:T(128)}, u32[]{:S(2)}) copy-start(s32[4]{0:T(128)} %live_ref.7) | copy-start | bytes 52
  517.6 41.3 %all-to-all-start.2 = ((bf16[8,4,32,768]{3,2,1,0:T(8,128)(2,1)}), bf16[8,4,32,768]{3,2,1,0:T(8,128)(2,1)S(1)}, u32[]{:S(2)}, u32[]{:S(2)}) async-start(bf16[8,4,32,768]{3,2,1,0:T(8,128)(2,1)} %bitcast.14), calls=%async_computation.2 | async-start | bytes 3145728 | tf_op jit(solution)/shard_map/all_to_all | solution.py:246
  558.9 41.3 %all-to-all-start = ((bf16[8,4,32,768]{3,2,1,0:T(8,128)(2,1)}), bf16[8,4,32,768]{3,2,1,0:T(8,128)(2,1)S(1)}, u32[]{:S(2)}, u32[]{:S(2)}) async-start(bf16[8,4,32,768]{3,2,1,0:T(8,128)(2,1)} %bitcast.7), calls=%async_computation | async-start | bytes 3145728 | tf_op jit(solution)/shard_map/all_to_all | solution.py:246
  562.9 2.8 copy-start.2
  565.7 58.9 %copy-start.1 = (s32[256]{0:T(256)S(1)}, s32[256]{0:T(256)}, u32[]{:S(2)}) copy-start(s32[256]{0:T(256)} %param.9) | copy-start | bytes 3076
  580.6 2.8 copy-start.3
  600.2 2.8 copy-start.4
  616.7 3.6 collective-permute-start.1
  620.4 3.6 collective-permute-start.2
Sparse Core Ops, SparseCore 0:
  12.2 327.9 all-gather.6
  341.9 182.7 all-gather.4
